TPU v7x, 32 devices: a whole 2x2x4 slice. The times are simulated.
32 devices in a mesh: groups: 2 (over x), blocks: 16 (over z, y, core).
Axes of the slice: x: 2, y: 2, z: 4, core: 2. Of those that a mesh axis runs over, the one named last changes fastest.
Arguments:
- features: bfloat16 [163840, 227], P(('groups', 'blocks')), parts along dimension 0, may hold values from -6 to 6
- pair_grid: int32 [16, 96], P('blocks'), may hold values from -4 to 43, as said below
- pair_slot: int32 [16, 96], P('blocks'), may hold values from 0 to 31, as said below
- slot_block: int32 [16, 32], P('blocks'), may hold values from -1 to 63, as said below
- pair_count: int32 [16], P('blocks'), may hold values from 24 to 96, as said below
- coupling: bfloat16 [16, 96, 128, 128], P('blocks'), may hold values from -0.3125 to 0.3125
- mesh_latent: bfloat16 [8192, 512], P('blocks'), may hold values from -6 to 6
- w_in: bfloat16 [227, 512], replicated, may hold values from -0.375 to 0.375
- b_in: float32 [512], replicated, may hold values from -3 to 3
- w_out: bfloat16 [512, 512], replicated, may hold values from -0.25 to 0.25
- b_out: float32 [512], replicated, may hold values from -3 to 3
- grid_gain: float32 [512], replicated, may hold values from 0.1 to 1.9
- w_edge: bfloat16 [512, 512], replicated, may hold values from -0.25 to 0.25
- w_mesh1: bfloat16 [1024, 512], replicated, may hold values from -0.1875 to 0.1875
- b_mesh1: float32 [512], replicated, may hold values from -3 to 3
- w_mesh2: bfloat16 [512, 512], replicated, may hold values from -0.25 to 0.25
- b_mesh2: float32 [512], replicated, may hold values from -3 to 3
- mesh_gain: float32 [512], replicated, may hold values from 0.1 to 1.9
Outputs:
- grid_latent: bfloat16 [163840, 512], P(('groups', 'blocks')), parts along dimension 0
- mesh_out: bfloat16 [16384, 512], P(('groups', 'blocks')), parts along dimension 0
There are 2 independent parts, one for each index of `groups`. A program takes and returns all parts, laid end to end along the dimension named above; an argument that names none is the same for every part. Nothing has to cross between parts.
Inputs may be any that keep to these rules, and one draw needn't show every extreme that they name: `pair_grid`: grid block offsets wrap around the band. `pair_slot`: every entry, live or not, names a slot whose mesh block is not -1. `slot_block`: slot s of a list holds -1 or a mesh block from (s // 2) * 4 to (s // 2 + 1) * 4 - 1; the mesh blocks of one list are distinct; every list has some s // 2 whose 2 slots are all filled. The live entries of a list are its first pair_count ones; some list has all 96.
All inputs are finite; a program needn't handle non-finite values.
Results may differ from a plain program's by a relative error of at most 0.006.
Values may be sent and summed in bfloat16 or wider, within the bound.
A program may use at most 256 MiB of HBM per device.

v0:
```python
import jax
import jax.numpy as jnp
from jax import lax
from jax.sharding import PartitionSpec as P

RIM = 4


norm_eps = 1e-05


def with_halo(cells, sides, width):
    for axis, dim in sides:
        count = lax.axis_size(axis)
        head = lax.slice_in_dim(cells, 0, width, axis=dim)
        tail = lax.slice_in_dim(cells, cells.shape[dim] - width, cells.shape[dim], axis=dim)
        cells = jnp.concatenate(
            [
                lax.ppermute(tail, axis, [(i, (i + 1) % count) for i in range(count)]),
                cells,
                lax.ppermute(head, axis, [((i + 1) % count, i) for i in range(count)]),
            ],
            axis=dim,
        )
    return cells


def layer_norm(values, gain):
    centred = values - jnp.mean(values, axis=-1, keepdims=True)
    spread = jnp.mean(centred * centred, axis=-1, keepdims=True)
    return centred * lax.rsqrt(spread + norm_eps) * gain


def on_device(
    features,
    pair_grid,
    pair_slot,
    slot_block,
    pair_count,
    coupling,
    mesh_latent,
    w_in,
    b_in,
    w_out,
    b_out,
    grid_gain,
    w_edge,
    w_mesh1,
    b_mesh1,
    w_mesh2,
    b_mesh2,
    mesh_gain,
):
    block_size = coupling.shape[-1]
    latent_width = w_edge.shape[1]
    pair_total = coupling.shape[1]
    activation = jax.nn.silu(
        jnp.dot(features, w_in, preferred_element_type=jnp.float32) + b_in
    ).astype(jnp.bfloat16)
    grid_latent = layer_norm(
        jnp.dot(activation, w_out, preferred_element_type=jnp.float32) + b_out, grid_gain
    ).astype(jnp.bfloat16)
    edge_rows = jnp.dot(grid_latent, w_edge, preferred_element_type=jnp.float32).astype(
        jnp.bfloat16
    )
    edge_blocks = edge_rows.reshape(-1, block_size, latent_width)
    padded = with_halo(edge_blocks, (("blocks", 0),), RIM)
    padded_count = padded.shape[0]
    slot_total = slot_block.shape[1]
    live_count = pair_count[0]
    grid_list = pair_grid[0] + RIM
    slot_list = pair_slot[0]
    coupling_list = coupling[0]
    grid_pick = (grid_list[:, None] == jnp.arange(padded_count, dtype=jnp.int32)[None, :]).astype(
        jnp.bfloat16
    )
    sources = jnp.dot(
        grid_pick, padded.reshape(padded_count, -1), preferred_element_type=jnp.float32
    ).astype(jnp.bfloat16)
    sources = sources.reshape(pair_total, block_size, latent_width)
    message = jnp.einsum("pqr,prf->pqf", coupling_list, sources, preferred_element_type=jnp.float32)
    alive_mask = jnp.arange(pair_total, dtype=jnp.int32) < live_count
    slot_pick = (
        (slot_list[None, :] == jnp.arange(slot_total, dtype=jnp.int32)[:, None])
        & alive_mask[None, :]
    ).astype(jnp.float32)
    partial_value = jnp.dot(
        slot_pick,
        message.reshape(pair_total, -1),
        precision=lax.Precision.HIGHEST,
        preferred_element_type=jnp.float32,
    )
    partial_value = partial_value.reshape(slot_total, block_size, latent_width)
    mesh_block_count = mesh_latent.shape[0] // block_size
    owner_total = lax.axis_size("blocks")
    send_sums = partial_value.reshape(
        owner_total, slot_total // owner_total, block_size, latent_width
    )
    send_ids = slot_block.reshape(owner_total, slot_total // owner_total)
    got_sums, got_ids = (
        lax.all_to_all(send_sums, "blocks", split_axis=0, concat_axis=0, tiled=True),
        lax.all_to_all(send_ids, "blocks", split_axis=0, concat_axis=0, tiled=True),
    )
    own_first = lax.axis_index("blocks") * mesh_block_count
    local_ids = jnp.where(got_ids >= 0, got_ids - own_first, mesh_block_count).reshape(-1)
    block_pick = (
        jnp.arange(mesh_block_count, dtype=jnp.int32)[:, None] == local_ids[None, :]
    ).astype(jnp.float32)
    received = got_sums.reshape(local_ids.shape[0], -1)
    aggregate = jnp.dot(
        block_pick, received, precision=lax.Precision.HIGHEST, preferred_element_type=jnp.float32
    ).reshape(-1, latent_width)
    aggregate_half = aggregate.astype(jnp.bfloat16)
    mesh_hidden = jax.nn.silu(
        jnp.dot(mesh_latent, w_mesh1[:latent_width], preferred_element_type=jnp.float32)
        + jnp.dot(aggregate_half, w_mesh1[latent_width:], preferred_element_type=jnp.float32)
        + b_mesh1
    ).astype(jnp.bfloat16)
    update = layer_norm(
        jnp.dot(mesh_hidden, w_mesh2, preferred_element_type=jnp.float32) + b_mesh2, mesh_gain
    )
    mesh_out = (mesh_latent.astype(jnp.float32) + update).astype(jnp.bfloat16)
    return (grid_latent, mesh_out)


def solution(mesh):
    in_specs = (
        P(("groups", "blocks"), None),
        P("blocks", None),
        P("blocks", None),
        P("blocks", None),
        P("blocks"),
        P("blocks", None, None, None),
        P("blocks", None),
        P(),
        P(),
        P(),
        P(),
        P(),
        P(),
        P(),
        P(),
        P(),
        P(),
        P(),
    )
    out_specs = (P(("groups", "blocks"), None), P(("groups", "blocks"), None))
    return jax.shard_map(
        on_device, mesh=mesh, in_specs=in_specs, out_specs=out_specs, check_vma=False
    )
```

profile of v0, /device:TPU:15, one launch (start us, length us, event | category | flops | bytes accessed | tf_op | source)
XLA Modules:
  0.0 343.5 jit_solution(5215559988963515497)
XLA Ops:
  0.6 0.0 copy-start
  0.6 0.0 copy-start.6
  0.7 10.1 %add_reduce_fusion = (f32[5120]{0:T(1024)S(1)}, f32[5120,512]{0,1:T(8,128)}) fusion(f32[512]{0:T(512)} %param.28, bf16[512,512]{1,0:T(8,128)(2,1)} %param.27, bf16[5120,227]{0,1:T(8,128)(2,1)} %param.18, bf16[227,512]{1,0:T(8,128)(2,1)} %param.25, f32[512]{0:T(512)} %param.26), kind=kOutput, calls=%fused_computation.8 | convolution fusion | flops 3895454720 | bytes 13591552 | tf_op jit(solution)/shard_map/dot_general | solution.py:61
  10.7 0.0 copy-start.7
  10.7 0.0 copy-done.6
  10.7 5.8 %multiply_reduce_fusion = f32[5120]{0:T(1024)S(1)} fusion(f32[5120,512]{0,1:T(8,128)} %get-tuple-element.11, f32[5120]{0:T(1024)S(1)} %broadcast_multiply_fusion, f32[512]{0:T(512)S(1)} %copy-done.6), kind=kLoop, calls=%fused_computation.6 | loop fusion | flops 10480640 | bytes 10528768 | tf_op jit(solution)/shard_map/reduce_sum | solution.py:30
  16.5 0.0 copy-start.10
  16.6 0.0 copy-done.7
  16.6 6.4 %multiply_convert_fusion = bf16[5120,512]{0,1:T(8,128)(2,1)S(1)} fusion(f32[5120,512]{0,1:T(8,128)} %get-tuple-element.11, f32[512]{0:T(512)S(1)} %copy-done.7, f32[5120]{0:T(1024)S(1)} %add_rsqrt_fusion, f32[5120]{0:T(1024)S(1)} %broadcast_multiply_fusion, f32[512]{0:T(512)S(1)} %copy-done.6), kind=kLoop, calls=%fused_computation.5 | loop fusion | flops 13107200 | bytes 15773696 | tf_op jit(solution)/shard_map/convert_element_type | solution.py:62
  23.0 0.0 copy-start.2
  23.0 2.4 copy-done.2
  25.4 0.0 copy-done.10
  25.4 0.0 copy-start.13
  25.4 0.0 copy-start.14
  25.4 3.2 convolution_convert_fusion.2
  28.6 0.0 copy-start.3
  28.6 2.3 copy-done.3
  30.9 1.0 fusion.28
  32.0 1.8 collective-permute-start
  33.8 0.0 collective-permute-start.1
  33.8 0.6 broadcast.116
  34.4 0.0 copy-done.13
  34.4 0.7 reduce.7
  35.1 0.7 all_to_all.9
  35.8 6.6 %all-to-all-start = ((s32[16,1,2]{2,1,0:T(1,128)}), s32[16,1,2]{2,1,0:T(1,128)S(1)}, u32[]{:S(2)}, u32[]{:S(2)}) async-start(s32[16,1,2]{2,1,0:T(1,128)} %bitcast), calls=%async_computation | async-start | bytes 16384 | tf_op jit(solution)/shard_map/all_to_all | solution.py:102
  42.4 7.6 %concatenate.11 = bf16[40,65536]{1,0:T(8,128)(2,1)} reshape(bf16[5120,512]{1,0:T(8,128)(2,1)} %copy-done.3) | data formatting | bytes 10485760 | tf_op jit(solution)/shard_map/concatenate | solution.py:17
  50.7 0.0 copy-done.14
  50.7 0.0 collective-permute-done
  50.7 1.4 copy.42
  52.1 0.0 collective-permute-done.1
  52.2 1.4 copy.43
  53.6 5.5 %convolution_convert_fusion = bf16[96,65536]{1,0:T(8,128)(2,1)S(1)} fusion(bf16[4,65536]{1,0:T(4,128)(2,1)S(1)} %bitcast.57, bf16[40,65536]{1,0:T(8,128)(2,1)} %concatenate.11, bf16[4,65536]{1,0:T(4,128)(2,1)S(1)} %bitcast.56, s32[96]{0:T(128)S(1)} %add_bitcast_fusion), kind=kOutput, calls=%fused_computation | convolution fusion | flops 629150208 | bytes 18874752 | tf_op jit(solution)/shard_map/dot_general | solution.py:77
  59.1 6.8 %copy.44 = bf16[12,8,128,512]{3,2,1,0:T(8,128)(2,1)} copy(bf16[12,8,128,512]{3,1,2,0:T(8,128)(2,1)S(1)} %bitcast.54) | data formatting | bytes 25165824
  65.8 0.0 copy-done
  65.8 12.9 %convolution_bitcast_fusion = f32[96,128,512]{1,2,0:T(8,128)} fusion(bf16[96,128,512]{2,1,0:T(8,128)(2,1)} %bitcast.53, bf16[1,96,128,128]{3,2,1,0:T(8,128)(2,1)S(1)} %copy-done), kind=kOutput, calls=%fused_computation.9 | convolution fusion | flops 1610612736 | bytes 40894464 | tf_op jit(solution)/shard_map/pqr,prf->pqf/dot_general | solution.py:81
  78.7 0.0 copy-start.9
  78.7 24.9 %copy.45 = f32[12,8,128,512]{3,1,2,0:T(8,128)} copy(f32[12,8,128,512]{2,3,1,0:T(8,128)} %bitcast.52) | data formatting | bytes 50331648
  103.6 0.0 copy-done.9
  103.6 16.0 %fusion = f32[16,2,128,512]{3,0,2,1:T(8,128)} fusion(s32[16,2]{0,1:T(2,128)S(1)} %multiply_add_fusion, s32[96]{0:T(128)S(1)} %bitcast.58, pred[96]{0:T(512)(128)(4,1)S(1)} %iota_compare_fusion.4, f32[12,8,128,512]{3,1,2,0:T(8,128)} %copy.45), kind=kOutput, calls=%fused_computation.3 | convolution fusion | flops 2415925248 | bytes 33555040 | tf_op jit(solution)/shard_map/dot_general | solution.py:87
  119.6 11.5 %copy.36 = f32[16,2,128,512]{3,2,1,0:T(8,128)} copy(f32[16,2,128,512]{3,0,2,1:T(8,128)} %fusion) | data formatting | bytes 16777216 | tf_op jit(solution)/shard_map/dot_general | solution.py:87
  131.1 0.0 copy-start.4
  131.1 0.0 copy-start.5
  131.1 0.0 all-to-all-done
  131.1 6.2 %all-to-all-start.1 = ((f32[16,2,128,512]{3,2,1,0:T(8,128)}), f32[16,2,128,512]{3,2,1,0:T(8,128)}, u32[]{:S(2)}, u32[]{:S(2)}) async-start(f32[16,2,128,512]{3,2,1,0:T(8,128)} %copy.36), calls=%async_computation.1 | async-start | bytes 16777216 | tf_op jit(solution)/shard_map/all_to_all | solution.py:101
  137.3 7.9 %copy.37 = bf16[5120,512]{1,0:T(8,128)(2,1)} copy(bf16[5120,512]{0,1:T(8,128)(2,1)} %copy-done.2) | data formatting | bytes 10485760
  145.2 0.0 copy-done.4
  145.2 1.0 copy.31
  146.2 0.0 copy-done.5
  146.2 1.4 fusion.14
  147.7 0.1 select_n.12
  147.8 171.9 %all-to-all-done.1 = f32[16,2,128,512]{3,2,1,0:T(8,128)} async-done(((f32[16,2,128,512]{3,2,1,0:T(8,128)}), f32[16,2,128,512]{3,2,1,0:T(8,128)}, u32[]{:S(2)}, u32[]{:S(2)}) %all-to-all-start.1) | async-done | bytes 8388640 | tf_op jit(solution)/shard_map/all_to_all | solution.py:101
  319.6 8.3 %copy.46 = f32[4,8,128,512]{3,1,2,0:T(8,128)S(1)} copy(f32[4,8,128,512]{3,2,1,0:T(8,128)} %bitcast.24) | data formatting | bytes 16777216
  327.9 0.0 copy-start.8
  327.9 0.0 copy-start.1
  327.9 3.8 %convolution_convert_fusion.1 = bf16[4,65536]{1,0:T(4,128)(2,1)} fusion(f32[32,65536]{1,0:T(8,128)S(1)} %bitcast.55, s32[32]{0:T(128)S(1)} %select_n.12), kind=kOutput, calls=%fused_computation.1 | convolution fusion | flops 100925568 | bytes 8913024 | tf_op jit(solution)/shard_map/dot_general | solution.py:110
  331.7 2.3 convert_element_type.36
  334.0 0.0 copy-done.11
  334.0 0.0 copy-done.12
  334.0 3.6 %fusion.29 = (f32[512]{0:T(512)S(1)}, f32[512,512]{0,1:T(8,128)}) fusion(f32[512]{0:T(512)S(1)} %copy-done.11, bf16[512,512]{1,0:T(8,128)(2,1)} %param.33, f32[512,512]{1,0:T(8,128)} %fusion.14, bf16[512,512]{1,0:T(8,128)(2,1)} %convert_element_type.36, f32[512]{0:T(512)S(1)} %copy-done.12, bf16[1024,512]{1,0:T(8,128)(2,1)} %param.31), kind=kOutput, calls=%fused_computation.52 | convolution fusion | flops 539229696 | bytes 3676160 | tf_op jit(solution)/shard_map/dot_general | solution.py:120
  337.6 1.4 multiply_reduce_fusion.1
  339.0 0.0 copy-done.8
  339.0 2.4 add_convert_fusion
  341.4 2.0 copy.38
  343.5 0.0 copy-done.1
  (10 shorter events, 0.1 us)
Async XLA Ops:
  0.6 65.2 %copy-start = (bf16[1,96,128,128]{3,2,1,0:T(8,128)(2,1)S(1)}, bf16[1,96,128,128]{3,2,1,0:T(8,128)(2,1)}, u32[]{:S(2)}) copy-start(bf16[1,96,128,128]{3,2,1,0:T(8,128)(2,1)} %param.23) | copy-start | bytes 9437188
  0.6 10.1 %copy-start.6 = (f32[512]{0:T(512)S(1)}, f32[512]{0:T(512)}, u32[]{:S(2)}) copy-start(f32[512]{0:T(512)} %param.28) | copy-start | bytes 6148
  10.7 5.8 %copy-start.7 = (f32[512]{0:T(512)S(1)}, f32[512]{0:T(512)}, u32[]{:S(2)}) copy-start(f32[512]{0:T(512)} %param.29) | copy-start | bytes 6148
  16.5 8.8 %copy-start.10 = (bf16[512,512]{1,0:T(8,128)(2,1)S(1)}, bf16[512,512]{1,0:T(8,128)(2,1)}, u32[]{:S(2)}) copy-start(bf16[512,512]{1,0:T(8,128)(2,1)} %param.30) | copy-start | bytes 1572868
  23.0 2.4 copy-start.2
  25.4 9.0 %copy-start.13 = (s32[1,32]{1,0:T(1,128)S(1)}, s32[1,32]{1,0:T(1,128)}, u32[]{:S(2)}) copy-start(s32[1,32]{1,0:T(1,128)} %param.21) | copy-start | bytes 388
  25.4 25.3 %copy-start.14 = (s32[1,96]{1,0:T(1,128)S(1)}, s32[1,96]{1,0:T(1,128)}, u32[]{:S(2)}) copy-start(s32[1,96]{1,0:T(1,128)} %param.19) | copy-start | bytes 1156
  28.6 2.4 copy-start.3
  32.0 18.7 %collective-permute-start = (bf16[4,128,512]{2,1,0:T(8,128)(2,1)}, bf16[4,128,512]{2,1,0:T(8,128)(2,1)}, u32[]{:S(2)}, u32[]{:S(2)}) collective-permute-start(bf16[4,128,512]{2,1,0:T(8,128)(2,1)} %bitcast.6), channel_id=1, source_target_pairs={{0,1},{1,2},{2,3},{3,4},{4,5},{5,6},{6,7},{7,8},{8,9},{9,10},{10,1... | collective-permute-start | bytes 1572872 | tf_op jit(solution)/shard_map/ppermute | solution.py:19
  33.8 18.4 %collective-permute-start.1 = (bf16[4,128,512]{2,1,0:T(8,128)(2,1)}, bf16[4,128,512]{2,1,0:T(8,128)(2,1)}, u32[]{:S(2)}, u32[]{:S(2)}) collective-permute-start(bf16[4,128,512]{2,1,0:T(8,128)(2,1)} %bitcast.7), channel_id=1, source_target_pairs={{1,0},{2,1},{3,2},{4,3},{5,4},{6,5},{7,6},{8,7},{9,8},{10,9},{11,1... | collective-permute-start | bytes 1572872 | tf_op jit(solution)/shard_map/ppermute | solution.py:21
  35.8 95.3 %all-to-all-start = ((s32[16,1,2]{2,1,0:T(1,128)}), s32[16,1,2]{2,1,0:T(1,128)S(1)}, u32[]{:S(2)}, u32[]{:S(2)}) async-start(s32[16,1,2]{2,1,0:T(1,128)} %bitcast), calls=%async_computation | async-start | bytes 16384 | tf_op jit(solution)/shard_map/all_to_all | solution.py:102
  78.7 24.9 %copy-start.9 = (s32[1,96]{1,0:T(1,128)S(1)}, s32[1,96]{1,0:T(1,128)}, u32[]{:S(2)}) copy-start(s32[1,96]{1,0:T(1,128)} %param.20) | copy-start | bytes 1156
  131.1 14.1 %copy-start.4 = (bf16[512,512]{1,0:T(8,128)(2,1)S(1)}, bf16[512,512]{1,0:T(8,128)(2,1)}, u32[]{:S(2)}) copy-start(bf16[512,512]{1,0:T(8,128)(2,1)} %param.24) | copy-start | bytes 1572868
  131.1 15.1 %copy-start.5 = (bf16[1024,512]{1,0:T(8,128)(2,1)S(1)}, bf16[1024,512]{1,0:T(8,128)(2,1)}, u32[]{:S(2)}) copy-start(bf16[1024,512]{1,0:T(8,128)(2,1)} %param.31) | copy-start | bytes 3145732
  131.1 188.5 %all-to-all-start.1 = ((f32[16,2,128,512]{3,2,1,0:T(8,128)}), f32[16,2,128,512]{3,2,1,0:T(8,128)}, u32[]{:S(2)}, u32[]{:S(2)}) async-start(f32[16,2,128,512]{3,2,1,0:T(8,128)} %copy.36), calls=%async_computation.1 | async-start | bytes 16777216 | tf_op jit(solution)/shard_map/all_to_all | solution.py:101
  319.6 14.3 %copy-start.11 = (f32[512]{0:T(512)S(1)}, f32[512]{0:T(512)}, u32[]{:S(2)}) copy-start(f32[512]{0:T(512)} %param.34) | copy-start | bytes 6148
  319.6 14.3 %copy-start.12 = (f32[512]{0:T(512)S(1)}, f32[512]{0:T(512)}, u32[]{:S(2)}) copy-start(f32[512]{0:T(512)} %param.32) | copy-start | bytes 6148
  327.9 11.1 %copy-start.8 = (f32[512]{0:T(512)S(1)}, f32[512]{0:T(512)}, u32[]{:S(2)}) copy-start(f32[512]{0:T(512)} %param.35) | copy-start | bytes 6148
  327.9 15.6 %copy-start.1 = (bf16[1,96,128,128]{3,2,1,0:T(8,128)(2,1)S(1)}, bf16[1,96,128,128]{3,2,1,0:T(8,128)(2,1)}, u32[]{:S(2)}) copy-start(bf16[1,96,128,128]{3,2,1,0:T(8,128)(2,1)} %param.23) | copy-start | bytes 9437188
where the time goes:
time: 345 us; the launch traced here: 343 us
  waiting for transfers between devices  172 us (50%)
  local copies, waits for them, and re-layouts  82.3 us (24%)
  matrix products  56.5 us (16%)
  other arithmetic  16.7 us (5%)
  starting transfers between devices  14.6 us (4%)
    all_to_all x1, waiting for transfers between devices, on_device(): lax.all_to_all(send_sums, 'blocks', split_axis=0, concat_axis=0, tiled=True)  172 us
    unnamed x39, local copies, waits for them, and re-layouts  59.1 us
    dot_general x1, matrix products, on_device(): jnp.dot(slot_pick, message.reshape(pair_total, -1), precision=lax.Precisi...  16 us
    dot_general x1, matrix products, on_device(): jnp.einsum('pqr,prf->pqf', coupling_list, sources, preferred_element_type...  12.9 us
    dot_general x1, local copies, waits for them, and re-layouts, on_device(): jnp.dot(slot_pick, message.reshape(pair_total, -1), precision=lax.Precisi...  11.5 us
    dot_general x1, matrix products, on_device(): jnp.dot(activation, w_out, preferred_element_type=jnp.float32) + b_out  10.1 us
    concatenate x1, local copies, waits for them, and re-layouts, with_halo(): jnp.concatenate([lax.ppermute(tail, axis, [(i, (i + 1) % count) for i in...  7.6 us
    reduce_sum x2, other arithmetic, layer_norm(): spread = jnp.mean(centred * centred, axis=-1, keepdims=True)  7.15 us
  transfers between devices with their start and end apart: 4, of which 1 were waited for; matrix products, arithmetic and copies ran while one was open for 29% of the time, Pallas kernels for 0%

commit v1 on v0

v1 whole, which is shorter than its diff:
```python
import functools

import jax
import jax.numpy as jnp
from jax import lax
from jax.experimental import pallas as pl
from jax.experimental.pallas import tpu as pltpu
from jax.sharding import PartitionSpec as P

RIM = 4

norm_eps = 1e-05
vmem_bytes = 56 * 1024 * 1024


def silu(values):
    return 0.5 * values * (1.0 + jnp.tanh(0.5 * values))


def layer_norm(values, gain):
    centred = values - jnp.mean(values, axis=-1, keepdims=True)
    spread = jnp.mean(centred * centred, axis=-1, keepdims=True)
    return centred * lax.rsqrt(spread + norm_eps) * gain


def grid_rows(features, w_in, b_in, w_out, b_out, grid_gain, w_edge):
    hidden = jnp.dot(features[...], w_in[...], preferred_element_type=jnp.float32) + b_in[...]
    activation = silu(hidden).astype(jnp.bfloat16)
    latent = jnp.dot(activation, w_out[...], preferred_element_type=jnp.float32) + b_out[...]
    latent = layer_norm(latent, grid_gain[...]).astype(jnp.bfloat16)
    edges = jnp.dot(latent, w_edge[...], preferred_element_type=jnp.float32).astype(jnp.bfloat16)
    return latent, edges


def rim_kernel(features, w_in, b_in, w_out, b_out, grid_gain, w_edge, latent_out, head, tail):
    latent, edges = grid_rows(features, w_in, b_in, w_out, b_out, grid_gain, w_edge)
    latent_out[...] = latent

    @pl.when(pl.program_id(0) == 0)
    def _():
        head[...] = edges

    @pl.when(pl.program_id(0) == 1)
    def _():
        tail[...] = edges


def inner_kernel(
    features, w_in, b_in, w_out, b_out, grid_gain, w_edge, rim_latent, latent_out, edges_out
):
    latent, edges = grid_rows(features, w_in, b_in, w_out, b_out, grid_gain, w_edge)
    latent_out[...] = latent
    edges_out[...] = edges


def pair_kernel(
    pair_grid,
    pair_slot,
    slot_block,
    pair_count,
    left,
    head,
    inner,
    tail,
    right,
    coupling,
    sums_out,
    edges,
    weights,
    acc,
    stage,
    load_sem,
    store_sem,
):
    pairs = weights.shape[0]
    blocks = stage.shape[0]
    inner_blocks = inner.shape[0]
    begin = 0
    loads = []
    for position, part in enumerate((left, head, inner, tail, right)):
        count = part.shape[0]
        loads.append(
            pltpu.make_async_copy(part, edges.at[pl.ds(begin, count)], load_sem.at[position])
        )
        begin += count
    loads.append(pltpu.make_async_copy(coupling.at[0], weights, load_sem.at[5]))
    for load in loads:
        load.start()

    @pl.loop(0, blocks)
    def _(block):
        acc[block] = jnp.zeros(acc.shape[1:], jnp.float32)

    for load in loads:
        load.wait()
    live = pair_count[0]
    unroll = 4

    @pl.loop(0, (live + unroll - 1) // unroll)
    def _(group):
        for lane in range(unroll):
            pair = group * unroll + lane
            target = slot_block[0, pair_slot[0, pair]]
            target = jnp.where(pair < live, target, blocks)
            acc[target] += jnp.dot(
                weights[pair],
                edges[pair_grid[0, pair] + RIM],
                preferred_element_type=jnp.float32,
            )

    piece = store_sem.shape[0]
    step = blocks // piece

    def store(index):
        span = pl.ds(index * step, step)
        return pltpu.make_async_copy(stage.at[span], sums_out.at[span], store_sem.at[index])

    @pl.loop(0, piece)
    def _(index):
        for offset in range(step):
            block = index * step + offset
            stage[block] = acc[block].astype(jnp.bfloat16)
        store(index).start()

    @pl.loop(0, piece)
    def _(index):
        store(index).wait()


def ring_kernel(
    device_total,
    sums,
    mesh_latent,
    w_mesh1,
    b_mesh1,
    w_mesh2,
    b_mesh2,
    mesh_gain,
    mesh_out,
    own,
    peer,
    got,
    hidden,
    own_sem,
    peer_send,
    peer_recv,
    ring_send,
    ring_recv,
):
    chips = device_total // 2
    per_owner = own.shape[1]
    half = per_owner // 2
    block_size = own.shape[2]
    width = own.shape[3]
    me = lax.axis_index("blocks")
    chip = me // 2
    core = me % 2

    def chip_at(place):
        return jnp.where(place < chips // 2, 2 * place, 2 * (chips - 1 - place) + 1)

    place = jnp.where(chip % 2 == 0, chip // 2, chips - 1 - chip // 2)
    after = 2 * chip_at((place + 1) % chips) + core
    before = 2 * chip_at((place + chips - 1) % chips) + core
    other = 2 * chip + 1 - core

    barrier = pltpu.get_barrier_semaphore()
    for device in (other, after, before):
        pl.semaphore_signal(
            barrier, inc=1, device_id={"blocks": device}, device_id_type=pl.DeviceIdType.MESH
        )

    def owner_chip(step, way):
        if way == 0:
            return chip_at((place + 2 * chips - 1 - step) % chips)
        return chip_at((place + 1 + step) % chips)

    def own_copy(step, way):
        first = (2 * owner_chip(step, way) + core) * per_owner + way * half
        return pltpu.make_async_copy(
            sums.at[pl.ds(first, half)],
            own.at[step, pl.ds(way * half, half)],
            own_sem.at[step, way],
        )

    def peer_copy(step, way):
        first = (2 * owner_chip(step, way) + 1 - core) * per_owner + way * half
        return pltpu.make_async_remote_copy(
            src_ref=sums.at[pl.ds(first, half)],
            dst_ref=peer.at[step, pl.ds(way * half, half)],
            send_sem=peer_send.at[step, way],
            recv_sem=peer_recv.at[step, way],
            device_id={"blocks": other},
            device_id_type=pl.DeviceIdType.MESH,
        )

    def ring_copy(step, chain):
        return pltpu.make_async_remote_copy(
            src_ref=own.at[step, chain],
            dst_ref=got.at[step, chain],
            send_sem=ring_send.at[step, chain],
            recv_sem=ring_recv.at[step, chain],
            device_id={"blocks": after if chain < half else before},
            device_id_type=pl.DeviceIdType.MESH,
        )

    ahead = 3

    @pl.loop(0, chips)
    def _(step):
        for way in range(2):
            own_copy(step, way).start()

    pl.semaphore_wait(barrier, 3)
    for step in range(ahead):
        for way in range(2):
            peer_copy(step, way).start()

    def both(step, chain):
        return own[step, chain].astype(jnp.float32) + peer[step, chain].astype(jnp.float32)

    def arrive(step):
        for way in range(2):
            own_copy(step, way).wait()
            peer_copy(step, way).wait_recv()

    order = [chain for pair in zip(range(half), range(half, per_owner)) for chain in pair]
    arrive(0)
    for chain in order:
        own[0, chain] = both(0, chain).astype(jnp.bfloat16)
        ring_copy(0, chain).start()

    hidden[...] = (
        jnp.dot(mesh_latent[...], w_mesh1[:width], preferred_element_type=jnp.float32)
        + b_mesh1[...]
    )

    @pl.loop(1, chips - 1)
    def _(step):
        @pl.when(step + ahead - 1 < chips)
        def _():
            for way in range(2):
                peer_copy(step + ahead - 1, way).start()

        arrive(step)
        for chain in order:
            ring_copy(step - 1, chain).wait_recv()
            total = both(step, chain) + got[step - 1, chain].astype(jnp.float32)
            own[step, chain] = total.astype(jnp.bfloat16)
            ring_copy(step, chain).start()

    last = chips - 1
    arrive(last)
    for chain in order:
        ring_copy(last - 1, chain).wait_recv()
        total = both(last, chain) + got[last - 1, chain].astype(jnp.float32)
        rows = pl.ds(chain * block_size, block_size)
        value = hidden[rows] + jnp.dot(
            total.astype(jnp.bfloat16), w_mesh1[width:], preferred_element_type=jnp.float32
        )
        value = silu(value).astype(jnp.bfloat16)
        value = jnp.dot(value, w_mesh2[...], preferred_element_type=jnp.float32) + b_mesh2[...]
        update = layer_norm(value, mesh_gain[...])
        mesh_out[rows] = (mesh_latent[rows].astype(jnp.float32) + update).astype(jnp.bfloat16)

    @pl.loop(0, chips)
    def _(step):
        for way in range(2):
            peer_copy(step, way).wait_send()

    @pl.loop(0, chips - 1)
    def _(step):
        for chain in range(per_owner):
            ring_copy(step, chain).wait_send()


def on_device(
    features,
    pair_grid,
    pair_slot,
    slot_block,
    pair_count,
    coupling,
    mesh_latent,
    w_in,
    b_in,
    w_out,
    b_out,
    grid_gain,
    w_edge,
    w_mesh1,
    b_mesh1,
    w_mesh2,
    b_mesh2,
    mesh_gain,
):
    block_size = coupling.shape[-1]
    pair_total = coupling.shape[1]
    width = w_edge.shape[1]
    rows, feature_width = features.shape
    tile = RIM * block_size
    tiles = rows // tile
    owner_total = lax.axis_size("blocks")
    own_blocks = mesh_latent.shape[0] // block_size
    mesh_blocks = own_blocks * owner_total
    bf16 = jnp.bfloat16
    f32 = jnp.float32

    def flat(vector):
        return vector.reshape(1, -1)

    params = (w_in, flat(b_in), w_out, flat(b_out), flat(grid_gain), w_edge)
    param_specs = [pl.BlockSpec(param.shape, lambda i: (0, 0)) for param in params]

    def cost(steps):
        work = 2 * tile * width * (feature_width + 2 * width)
        return pl.CostEstimate(
            flops=steps * work,
            bytes_accessed=steps * tile * (feature_width + 2 * width) * 2,
            transcendentals=steps * tile * width,
        )

    whole_tile = pl.BlockSpec((tile, width), lambda i: (0, 0))
    rim_latent, head, tail = pl.pallas_call(
        rim_kernel,
        grid=(2,),
        in_specs=[pl.BlockSpec((tile, feature_width), lambda i: (i * (tiles - 1), 0))]
        + param_specs,
        out_specs=[
            pl.BlockSpec((tile, width), lambda i: (i * (tiles - 1), 0)),
            whole_tile,
            whole_tile,
        ],
        out_shape=[
            jax.ShapeDtypeStruct((rows, width), bf16),
            jax.ShapeDtypeStruct((tile, width), bf16),
            jax.ShapeDtypeStruct((tile, width), bf16),
        ],
        cost_estimate=cost(2),
        compiler_params=pltpu.CompilerParams(vmem_limit_bytes=vmem_bytes),
        name="rim_rows",
    )(features, *params)

    left = lax.ppermute(tail, "blocks", [(i, (i + 1) % owner_total) for i in range(owner_total)])
    right = lax.ppermute(head, "blocks", [((i + 1) % owner_total, i) for i in range(owner_total)])

    grid_latent, inner = pl.pallas_call(
        inner_kernel,
        grid=(tiles - 2,),
        in_specs=[pl.BlockSpec((tile, feature_width), lambda i: (i + 1, 0))]
        + param_specs
        + [pl.BlockSpec(memory_space=pl.ANY)],
        out_specs=[
            pl.BlockSpec((tile, width), lambda i: (i + 1, 0)),
            pl.BlockSpec((tile, width), lambda i: (i, 0)),
        ],
        out_shape=[
            jax.ShapeDtypeStruct((rows, width), bf16),
            jax.ShapeDtypeStruct((rows - 2 * tile, width), bf16),
        ],
        input_output_aliases={7: 0},
        cost_estimate=cost(tiles - 2),
        compiler_params=pltpu.CompilerParams(vmem_limit_bytes=vmem_bytes),
        name="inner_rows",
    )(features, *params, rim_latent)

    edge_parts = [
        part.reshape(-1, block_size, width) for part in (left, head, inner, tail, right)
    ]
    edge_total = sum(part.shape[0] for part in edge_parts)
    smem = pl.BlockSpec(memory_space=pltpu.SMEM)
    anywhere = pl.BlockSpec(memory_space=pl.ANY)
    sums = pl.pallas_call(
        pair_kernel,
        in_specs=[smem] * 4 + [anywhere] * 6,
        out_specs=anywhere,
        out_shape=jax.ShapeDtypeStruct((mesh_blocks, block_size, width), bf16),
        scratch_shapes=[
            pltpu.VMEM((edge_total, block_size, width), bf16),
            pltpu.VMEM((pair_total, block_size, block_size), bf16),
            pltpu.VMEM((mesh_blocks + 1, block_size, width), f32),
            pltpu.VMEM((mesh_blocks, block_size, width), bf16),
            pltpu.SemaphoreType.DMA((6,)),
            pltpu.SemaphoreType.DMA((owner_total,)),
        ],
        compiler_params=pltpu.CompilerParams(vmem_limit_bytes=62 * 1024 * 1024),
        name="pair_sums",
    )(pair_grid, pair_slot, slot_block, pair_count, *edge_parts, coupling)

    chips = owner_total // 2
    vmem = pl.BlockSpec(memory_space=pltpu.VMEM)
    mesh_out = pl.pallas_call(
        functools.partial(ring_kernel, owner_total),
        in_specs=[anywhere] + [vmem] * 6,
        out_specs=vmem,
        out_shape=jax.ShapeDtypeStruct(mesh_latent.shape, bf16),
        scratch_shapes=[
            pltpu.VMEM((chips, own_blocks, block_size, width), bf16),
            pltpu.VMEM((chips, own_blocks, block_size, width), bf16),
            pltpu.VMEM((chips - 1, own_blocks, block_size, width), bf16),
            pltpu.VMEM(mesh_latent.shape, f32),
            pltpu.SemaphoreType.DMA((chips, 2)),
            pltpu.SemaphoreType.DMA((chips, 2)),
            pltpu.SemaphoreType.DMA((chips, 2)),
            pltpu.SemaphoreType.DMA((chips - 1, own_blocks)),
            pltpu.SemaphoreType.DMA((chips - 1, own_blocks)),
        ],
        compiler_params=pltpu.CompilerParams(
            collective_id=0, has_side_effects=True, vmem_limit_bytes=vmem_bytes
        ),
        name="ring_sums",
    )(sums, mesh_latent, w_mesh1, flat(b_mesh1), w_mesh2, flat(b_mesh2), flat(mesh_gain))
    return (grid_latent, mesh_out)


def solution(mesh):
    in_specs = (
        P(("groups", "blocks"), None),
        P("blocks", None),
        P("blocks", None),
        P("blocks", None),
        P("blocks"),
        P("blocks", None, None, None),
        P("blocks", None),
        P(),
        P(),
        P(),
        P(),
        P(),
        P(),
        P(),
        P(),
        P(),
        P(),
        P(),
    )
    out_specs = (P(("groups", "blocks"), None), P(("groups", "blocks"), None))
    return jax.shard_map(
        on_device, mesh=mesh, in_specs=in_specs, out_specs=out_specs, check_vma=False
    )
```

time: 345 us -> 93.1 us (0.27)
  the two profiles are of different devices: /device:TPU:15 before, /device:TPU:0 now
where the time goes in v1:
time: 93.1 us; the launch traced here: 92.2 us
  Pallas kernels  78.2 us (84%)
  local copies, waits for them, and re-layouts  7.16 us (8%)
  starting transfers between devices  5.5 us (6%)
  between operations  1.32 us (1%)
    pallas_call x1, Pallas kernels, on_device(): pl.pallas_call(functools.partial(ring_kernel, owner_total), in_specs=[any...  51.1 us
    pallas_call x1, Pallas kernels, on_device(): pl.pallas_call(inner_kernel, grid=(tiles - 2,), in_specs=[pl.BlockSpec((t...  12 us
    pallas_call x1, Pallas kernels, on_device(): pl.pallas_call(pair_kernel, in_specs=[smem] * 4 + [anywhere] * 6, out_spe...  9.95 us
    unnamed x6, local copies, waits for them, and re-layouts  7.16 us
    pallas_call x1, Pallas kernels, on_device(): pl.pallas_call(rim_kernel, grid=(2,), in_specs=[pl.BlockSpec((tile, featu...  5.12 us
    ppermute x1, starting transfers between devices, on_device(): lax.ppermute(head, 'blocks', [((i + 1) % owner_total, i) for i in range(o...  5.05 us
  transfers between devices with their start and end apart: 2, of which 0 were waited for; matrix products, arithmetic and copies ran while one was open for 0% of the time, Pallas kernels for 13%

profile of v1, /device:TPU:0, one launch (start us, length us, event | category | flops | bytes accessed | tf_op | source)
XLA Modules:
  0.0 92.2 jit_solution(11776472436912895991)
XLA Ops:
  0.6 4.3 %copy.22.features = bf16[5120,227]{1,0:T(8,128)(2,1)} copy(bf16[5120,227]{0,1:T(8,128)(2,1)} %param.18) | data formatting | bytes 4648960 | tf_op args[0]
  5.0 5.1 %rim_rows.1 = (bf16[5120,512]{1,0:T(8,128)(2,1)}, bf16[512,512]{1,0:T(8,128)(2,1)}, bf16[512,512]{1,0:T(8,128)(2,1)}) custom-call(bf16[5120,227]{1,0:T(8,128)(2,1)} %copy.22.features, bf16[227,512]{1,0:T(8,128)(2,1)} %w_in.3, f32[1,512]{1,0:T(1,128)} %bitcast.19, bf16[512,512]{1,0:T(8,128)(2,1)} %w_out.3, f32[1,512]{1,0:T(1,128)} %bitcast.21, ...), custom_call_target="tpu_custom_call" | custom-call | flops 1311768576 | bytes 2562048 | tf_op jit(solution)/shard_map/rim_rows/pallas_call | solution.py:324
  10.1 0.4 collective-permute-start
  10.5 5.0 %collective-permute-start.1 = (bf16[512,512]{1,0:T(8,128)(2,1)}, bf16[512,512]{1,0:T(8,128)(2,1)S(1)}, u32[]{:S(2)}, u32[]{:S(2)}) collective-permute-start(bf16[512,512]{1,0:T(8,128)(2,1)} %get-tuple-element.10), channel_id=1, source_target_pairs={{1,0},{2,1},{3,2},{4,3},{5,4},{6,5},{7,6},{8,7},{9,8},{10,9},{11,1... | collective-permute-start | bytes 1572872 | tf_op jit(solution)/shard_map/ppermute | solution.py:345
  16.2 12.0 %inner_rows.1 = (bf16[5120,512]{1,0:T(8,128)(2,1)}, bf16[4096,512]{1,0:T(8,128)(2,1)}) custom-call(bf16[5120,227]{1,0:T(8,128)(2,1)} %copy.22.features, bf16[227,512]{1,0:T(8,128)(2,1)} %w_in.3, f32[1,512]{1,0:T(1,128)} %bitcast.20, bf16[512,512]{1,0:T(8,128)(2,1)} %w_out.3, f32[1,512]{1,0:T(1,128)} %bitcast.22, ...), custom_call_target="tpu_custom_call", output_to_operand_aliasing={{0}: (7, {})} | custom-call | flops 5247074304 | bytes 10248192 | tf_op jit(solution)/shard_map/inner_rows/pallas_call | solution.py:347
  28.2 0.0 collective-permute-done
  28.3 0.0 copy-start
  28.3 0.0 collective-permute-done.1
  28.3 0.0 copy-start.1
  28.3 0.8 copy-done
  29.1 0.2 copy-done.1
  29.2 10.0 %pair_sums.1.sums = bf16[64,128,512]{2,1,0:T(8,128)(2,1)} custom-call(s32[1,96]{1,0:T(1,128)} %pair_grid.1, s32[1,96]{1,0:T(1,128)} %pair_slot.1, s32[1,32]{1,0:T(1,128)} %slot_block.1, s32[1]{0:T(128)S(6)} %copy.25.pair_count, bf16[4,128,512]{2,1,0:T(8,128)(2,1)} %bitcast.14, bf16[4,128,512]{2,1,0:T(8,128)(2,1)} %bitcast.12, ...), custom_call_target="tpu_custom_call" | custom-call | tf_op jit(solution)/shard_map/pair_sums/pallas_call | solution.py:373
  39.2 51.1 %ring_sums.1 = bf16[512,512]{1,0:T(8,128)(2,1)} custom-call(bf16[64,128,512]{2,1,0:T(8,128)(2,1)} %pair_sums.1.sums, bf16[512,512]{1,0:T(8,128)(2,1)} %mesh_latent.1, bf16[1024,512]{1,0:T(8,128)(2,1)} %w_mesh1.1, f32[1,512]{1,0:T(1,128)} %bitcast.16, bf16[512,512]{1,0:T(8,128)(2,1)} %w_mesh2.1, f32[1,512]{1,0:T(1,128)} %bitcast.17, f32[1,512]{1,0:T(1,128)} %bitcast.18), custom_call_target="tpu_custom_call" | custom-call | tf_op jit(solution)/shard_map/ring_sums/pallas_call | solution.py:392
  90.3 1.9 %copy.26 = bf16[512,512]{1,0:T(8,128)(2,1)} copy(bf16[512,512]{1,0:T(8,128)(2,1)} %ring_sums.1) | data formatting | bytes 1048576
Async XLA Ops:
  10.1 18.2 %collective-permute-start = (bf16[512,512]{1,0:T(8,128)(2,1)}, bf16[512,512]{1,0:T(8,128)(2,1)S(1)}, u32[]{:S(2)}, u32[]{:S(2)}) collective-permute-start(bf16[512,512]{1,0:T(8,128)(2,1)} %get-tuple-element.9), channel_id=1, source_target_pairs={{0,1},{1,2},{2,3},{3,4},{4,5},{5,6},{6,7},{7,8},{8,9},{9,10},{10,1... | collective-permute-start | bytes 1572872 | tf_op jit(solution)/shard_map/ppermute | solution.py:344
  10.5 17.7 %collective-permute-start.1 = (bf16[512,512]{1,0:T(8,128)(2,1)}, bf16[512,512]{1,0:T(8,128)(2,1)S(1)}, u32[]{:S(2)}, u32[]{:S(2)}) collective-permute-start(bf16[512,512]{1,0:T(8,128)(2,1)} %get-tuple-element.10), channel_id=1, source_target_pairs={{1,0},{2,1},{3,2},{4,3},{5,4},{6,5},{7,6},{8,7},{9,8},{10,9},{11,1... | collective-permute-start | bytes 1572872 | tf_op jit(solution)/shard_map/ppermute | solution.py:345
  28.3 0.8 copy-start
  28.3 1.0 %copy-start.1 = (bf16[512,512]{1,0:T(8,128)(2,1)}, bf16[512,512]{1,0:T(8,128)(2,1)S(1)}, u32[]{:S(2)}) copy-start(bf16[512,512]{1,0:T(8,128)(2,1)S(1)} %collective-permute-done.1) | copy-start | bytes 1572868

commit v2 on v1

v2 whole, which is shorter than its diff:
```python
import functools

import jax
import jax.numpy as jnp
from jax import lax
from jax.experimental import pallas as pl
from jax.experimental.pallas import tpu as pltpu
from jax.sharding import PartitionSpec as P

RIM = 4
cap = 2

norm_eps = 1e-05
vmem_bytes = 56 * 1024 * 1024
chain_rows = 128
unroll = 8


def silu(values):
    return 0.5 * values * (1.0 + jnp.tanh(0.5 * values))


def layer_norm(values, gain):
    centred = values - jnp.mean(values, axis=-1, keepdims=True)
    spread = jnp.mean(centred * centred, axis=-1, keepdims=True)
    return centred * lax.rsqrt(spread + norm_eps) * gain


def grid_rows(features, w_in, b_in, w_out, b_out, grid_gain, w_edge):
    hidden = lax.dot_general(
        features, w_in[...], (((0,), (0,)), ((), ())), preferred_element_type=jnp.float32
    )
    activation = silu(hidden + b_in[...]).astype(jnp.bfloat16)
    latent = jnp.dot(activation, w_out[...], preferred_element_type=jnp.float32) + b_out[...]
    latent = layer_norm(latent, grid_gain[...]).astype(jnp.bfloat16)
    edges = jnp.dot(latent, w_edge[...], preferred_element_type=jnp.float32).astype(jnp.bfloat16)
    return latent, edges


def grid_kernel(
    features, w_in, b_in, w_out, b_out, grid_gain, w_edge, latent_out, edges_out
):
    latent, edges = grid_rows(features[...], w_in, b_in, w_out, b_out, grid_gain, w_edge)
    latent_out[...] = latent
    edges_out[...] = edges


def pair_kernel(
    pair_grid,
    pair_slot,
    slot_block,
    pair_count,
    features,
    w_in,
    b_in,
    w_out,
    b_out,
    grid_gain,
    w_edge,
    left,
    right,
    done,
    coupling,
    latent_in,
    latent_out,
    sums_out,
    edges,
    weights,
    acc,
    stage,
    zeros,
    held,
    load_sem,
    store_sem,
    latent_sem,
):
    slots = stage.shape[0]
    block_size, width = zeros.shape
    blocks = sums_out.shape[0]
    owners = slots // cap
    per_owner = blocks // owners
    rest = held.shape[0]
    rim = left.shape[1]
    done_rows = done.shape[0]
    loads = [
        pltpu.make_async_copy(coupling.at[0], weights, load_sem.at[0]),
        pltpu.make_async_copy(done, edges.at[pl.ds(rim, done_rows)], load_sem.at[1]),
    ]
    for load in loads:
        load.start()

    zeros[...] = jnp.zeros(zeros.shape, jnp.bfloat16)

    @pl.loop(0, owners)
    def _(owner):
        for offset in range(per_owner):
            block = owner * per_owner + offset
            used = slot_block[0, owner * cap] == block
            for extra in range(1, cap):
                used = used | (slot_block[0, owner * cap + extra] == block)

            @pl.when(jnp.logical_not(used))
            def _():
                pltpu.make_async_copy(zeros, sums_out.at[block], store_sem.at[block]).start()

    @pl.loop(0, slots)
    def _(slot):
        acc[slot] = jnp.zeros(acc.shape[1:], jnp.float32)

    params = (w_in, b_in, w_out, b_out, grid_gain, w_edge)
    latent, rest_edges = grid_rows(features[...], *params)
    held[...] = latent
    latent_copy = pltpu.make_async_copy(
        held, latent_out.at[pl.ds(done_rows, rest)], latent_sem
    )
    latent_copy.start()
    edges[pl.ds(rim + done_rows, rest)] = rest_edges
    unused, rim_edges = grid_rows(
        jnp.concatenate([left[...], right[...]], axis=1), *params
    )
    edges[pl.ds(0, rim)] = rim_edges[:rim]
    edges[pl.ds(rim + done_rows + rest, rim)] = rim_edges[rim:]

    for load in loads:
        load.wait()
    live = pair_count[0]

    @pl.loop(0, (live + unroll - 1) // unroll)
    def _(group):
        for lane in range(unroll):
            pair = group * unroll + lane
            target = jnp.where(pair < live, pair_slot[0, pair], slots)
            first = pl.multiple_of((pair_grid[0, pair] + RIM) * block_size, block_size)
            acc[target] += jnp.dot(
                weights[pair],
                edges[pl.ds(first, block_size)],
                preferred_element_type=jnp.float32,
            )

    @pl.loop(0, slots)
    def _(slot):
        stage[slot] = acc[slot].astype(jnp.bfloat16)
        block = slot_block[0, slot]

        @pl.when(block >= 0)
        def _():
            pltpu.make_async_copy(
                stage.at[slot], sums_out.at[block], store_sem.at[block]
            ).start()

    latent_copy.wait()

    @pl.loop(0, blocks)
    def _(block):
        pltpu.make_async_copy(zeros, sums_out.at[block], store_sem.at[block]).wait()


def ring_kernel(
    device_total,
    sums,
    mesh_latent,
    w_mesh1,
    b_mesh1,
    w_mesh2,
    b_mesh2,
    mesh_gain,
    mesh_out,
    own,
    peer,
    got,
    hidden,
    own_sem,
    peer_send,
    peer_recv,
    ring_send,
    ring_recv,
):
    chips = device_total // 2
    per_owner = own.shape[1]
    half = per_owner // 2
    width = own.shape[2]
    chains = per_owner // chain_rows
    me = lax.axis_index("blocks")
    chip = me // 2
    core = me % 2

    def chip_at(place):
        return jnp.where(place < chips // 2, 2 * place, 2 * (chips - 1 - place) + 1)

    place = jnp.where(chip % 2 == 0, chip // 2, chips - 1 - chip // 2)
    after = 2 * chip_at((place + 1) % chips) + core
    before = 2 * chip_at((place + chips - 1) % chips) + core
    other = 2 * chip + 1 - core

    barrier = pltpu.get_barrier_semaphore()
    for device in (other, after, before):
        pl.semaphore_signal(
            barrier, inc=1, device_id={"blocks": device}, device_id_type=pl.DeviceIdType.MESH
        )

    def owner_chip(step, way):
        if way == 0:
            return chip_at((place + 2 * chips - 1 - step) % chips)
        return chip_at((place + 1 + step) % chips)

    def own_copy(step, way):
        first = (2 * owner_chip(step, way) + core) * per_owner + way * half
        return pltpu.make_async_copy(
            sums.at[pl.ds(first, half)],
            own.at[step, pl.ds(way * half, half)],
            own_sem.at[step, way],
        )

    def peer_copy(step, way):
        first = (2 * owner_chip(step, way) + 1 - core) * per_owner + way * half
        return pltpu.make_async_remote_copy(
            src_ref=sums.at[pl.ds(first, half)],
            dst_ref=peer.at[step, pl.ds(way * half, half)],
            send_sem=peer_send.at[step, way],
            recv_sem=peer_recv.at[step, way],
            device_id={"blocks": other},
            device_id_type=pl.DeviceIdType.MESH,
        )

    def rows_of(chain):
        return pl.ds(chain * chain_rows, chain_rows)

    def ring_copy(step, chain):
        return pltpu.make_async_remote_copy(
            src_ref=own.at[step, rows_of(chain)],
            dst_ref=got.at[step, rows_of(chain)],
            send_sem=ring_send.at[step, chain],
            recv_sem=ring_recv.at[step, chain],
            device_id={"blocks": after if chain < chains // 2 else before},
            device_id_type=pl.DeviceIdType.MESH,
        )

    ahead = 3

    @pl.loop(0, chips)
    def _(step):
        for way in range(2):
            own_copy(step, way).start()

    pl.semaphore_wait(barrier, 3)
    for step in range(ahead):
        for way in range(2):
            peer_copy(step, way).start()

    def both(step, chain):
        rows = rows_of(chain)
        return own[step, rows].astype(jnp.float32) + peer[step, rows].astype(jnp.float32)

    def arrive(step):
        for way in range(2):
            own_copy(step, way).wait()
            peer_copy(step, way).wait_recv()

    order = [
        chain for pair in zip(range(chains // 2), range(chains // 2, chains)) for chain in pair
    ]
    arrive(0)
    for chain in order:
        own[0, rows_of(chain)] = both(0, chain).astype(jnp.bfloat16)
        ring_copy(0, chain).start()

    hidden[...] = (
        jnp.dot(mesh_latent[...], w_mesh1[:width], preferred_element_type=jnp.float32)
        + b_mesh1[...]
    )

    @pl.loop(1, chips - 1)
    def _(step):
        @pl.when(step + ahead - 1 < chips)
        def _():
            for way in range(2):
                peer_copy(step + ahead - 1, way).start()

        arrive(step)
        for chain in order:
            ring_copy(step - 1, chain).wait_recv()
            total = both(step, chain) + got[step - 1, rows_of(chain)].astype(jnp.float32)
            own[step, rows_of(chain)] = total.astype(jnp.bfloat16)
            ring_copy(step, chain).start()

    last = chips - 1
    arrive(last)
    for chain in order:
        ring_copy(last - 1, chain).wait_recv()
        total = both(last, chain) + got[last - 1, rows_of(chain)].astype(jnp.float32)
        rows = rows_of(chain)
        value = hidden[rows] + jnp.dot(
            total.astype(jnp.bfloat16), w_mesh1[width:], preferred_element_type=jnp.float32
        )
        value = silu(value).astype(jnp.bfloat16)
        value = jnp.dot(value, w_mesh2[...], preferred_element_type=jnp.float32) + b_mesh2[...]
        update = layer_norm(value, mesh_gain[...])
        mesh_out[rows] = (mesh_latent[rows].astype(jnp.float32) + update).astype(jnp.bfloat16)

    @pl.loop(0, chips)
    def _(step):
        for way in range(2):
            peer_copy(step, way).wait_send()

    @pl.loop(0, chips - 1)
    def _(step):
        for chain in range(chains):
            ring_copy(step, chain).wait_send()


def on_device(
    features,
    pair_grid,
    pair_slot,
    slot_block,
    pair_count,
    coupling,
    mesh_latent,
    w_in,
    b_in,
    w_out,
    b_out,
    grid_gain,
    w_edge,
    w_mesh1,
    b_mesh1,
    w_mesh2,
    b_mesh2,
    mesh_gain,
):
    block_size = coupling.shape[-1]
    pair_total = coupling.shape[1]
    width = w_edge.shape[1]
    rows, feature_width = features.shape
    tile = RIM * block_size
    tiles = rows // tile
    owner_total = lax.axis_size("blocks")
    slot_total = slot_block.shape[1]
    features = features.T
    own_blocks = mesh_latent.shape[0] // block_size
    mesh_blocks = own_blocks * owner_total
    bf16 = jnp.bfloat16
    f32 = jnp.float32

    def flat(vector):
        return vector.reshape(1, -1)

    params = (w_in, flat(b_in), w_out, flat(b_out), flat(grid_gain), w_edge)
    param_specs = [pl.BlockSpec(param.shape, lambda i: (0, 0)) for param in params]
    wide = 2 * tile
    done_steps = rows // wide - 1
    smem = pl.BlockSpec(memory_space=pltpu.SMEM)
    anywhere = pl.BlockSpec(memory_space=pl.ANY)
    vmem = pl.BlockSpec(memory_space=pltpu.VMEM)
    semaphore = pltpu.SemaphoreType.DMA
    count = done_steps * wide

    left = lax.ppermute(
        features[:, rows - tile :],
        "blocks",
        [(i, (i + 1) % owner_total) for i in range(owner_total)],
    )
    right = lax.ppermute(
        features[:, :tile], "blocks", [((i + 1) % owner_total, i) for i in range(owner_total)]
    )

    latent, done = pl.pallas_call(
        grid_kernel,
        grid=(done_steps,),
        in_specs=[pl.BlockSpec((feature_width, wide), lambda i: (0, i))] + param_specs,
        out_specs=[
            pl.BlockSpec((wide, width), lambda i: (i, 0)),
            pl.BlockSpec((wide, width), lambda i: (i, 0)),
        ],
        out_shape=[
            jax.ShapeDtypeStruct((rows, width), bf16),
            jax.ShapeDtypeStruct((count, width), bf16),
        ],
        cost_estimate=pl.CostEstimate(
            flops=count * 2 * width * (feature_width + 2 * width),
            bytes_accessed=count * (feature_width + 2 * width) * 2,
            transcendentals=count * width,
        ),
        compiler_params=pltpu.CompilerParams(vmem_limit_bytes=vmem_bytes),
        name="grid_rows",
    )(features, *params)

    grid_latent, sums = pl.pallas_call(
        pair_kernel,
        grid=(1,),
        in_specs=[smem] * 4
        + [pl.BlockSpec((feature_width, wide), lambda i: (0, done_steps))]
        + param_specs
        + [vmem, vmem, anywhere, anywhere, anywhere],
        out_specs=[anywhere, anywhere],
        out_shape=[
            jax.ShapeDtypeStruct((rows, width), bf16),
            jax.ShapeDtypeStruct((mesh_blocks, block_size, width), bf16),
        ],
        scratch_shapes=[
            pltpu.VMEM((rows + 2 * tile, width), bf16),
            pltpu.VMEM((pair_total, block_size, block_size), bf16),
            pltpu.VMEM((slot_total + 1, block_size, width), f32),
            pltpu.VMEM((slot_total, block_size, width), bf16),
            pltpu.VMEM((block_size, width), bf16),
            pltpu.VMEM((wide, width), bf16),
            semaphore((2,)),
            semaphore((mesh_blocks,)),
            semaphore,
        ],
        input_output_aliases={15: 0},
        compiler_params=pltpu.CompilerParams(vmem_limit_bytes=vmem_bytes),
        name="pair_sums",
    )(
        pair_grid,
        pair_slot,
        slot_block,
        pair_count,
        features,
        *params,
        left,
        right,
        done,
        coupling,
        latent,
    )

    chips = owner_total // 2
    mesh_rows = own_blocks * block_size
    mesh_out = pl.pallas_call(
        functools.partial(ring_kernel, owner_total),
        in_specs=[anywhere] + [vmem] * 6,
        out_specs=vmem,
        out_shape=jax.ShapeDtypeStruct(mesh_latent.shape, bf16),
        scratch_shapes=[
            pltpu.VMEM((chips, mesh_rows, width), bf16),
            pltpu.VMEM((chips, mesh_rows, width), bf16),
            pltpu.VMEM((chips - 1, mesh_rows, width), bf16),
            pltpu.VMEM(mesh_latent.shape, f32),
            pltpu.SemaphoreType.DMA((chips, 2)),
            pltpu.SemaphoreType.DMA((chips, 2)),
            pltpu.SemaphoreType.DMA((chips, 2)),
            pltpu.SemaphoreType.DMA((chips - 1, mesh_rows // chain_rows)),
            pltpu.SemaphoreType.DMA((chips - 1, mesh_rows // chain_rows)),
        ],
        compiler_params=pltpu.CompilerParams(
            collective_id=0, has_side_effects=True, vmem_limit_bytes=vmem_bytes
        ),
        name="ring_sums",
    )(sums.reshape(-1, width), mesh_latent, w_mesh1, flat(b_mesh1), w_mesh2, flat(b_mesh2), flat(mesh_gain))
    return (grid_latent, mesh_out)


def solution(mesh):
    in_specs = (
        P(("groups", "blocks"), None),
        P("blocks", None),
        P("blocks", None),
        P("blocks", None),
        P("blocks"),
        P("blocks", None, None, None),
        P("blocks", None),
        P(),
        P(),
        P(),
        P(),
        P(),
        P(),
        P(),
        P(),
        P(),
        P(),
        P(),
    )
    out_specs = (P(("groups", "blocks"), None), P(("groups", "blocks"), None))
    return jax.shard_map(
        on_device, mesh=mesh, in_specs=in_specs, out_specs=out_specs, check_vma=False
    )
```

time: 93.1 us -> 83.9 us (0.901); the launches traced: 92.2 us -> 84.5 us
  Pallas kernels: 78.2 us -> 73.9 us
  local copies, waits for them, and re-layouts: 7.16 us -> 3.7 us
    unnamed x6 -> x5, local copies, waits for them, and re-layouts: 7.16 us -> 2.61 us
    pallas_call x3 -> x2, Pallas kernels: 27.1 us -> 22.7 us  [the longest x1 11.8 us: on_device(): pl.pallas_call(pair_kernel, grid=(1,), in_specs=[smem] * 4 + [pl.BlockSpe...]
    slice x0 -> x1, local copies, waits for them, and re-layouts: none -> 1.09 us  [on_device(): features[:, :tile]]
where the time goes in v2:
time: 83.9 us; the launch traced here: 84.5 us
  Pallas kernels  73.9 us (88%)
  starting transfers between devices  5.5 us (7%)
  local copies, waits for them, and re-layouts  3.7 us (4%)
  between operations  1.33 us (2%)
    pallas_call x1, Pallas kernels, on_device(): pl.pallas_call(functools.partial(ring_kernel, owner_total), in_specs=[any...  51.2 us
    pallas_call x1, Pallas kernels, on_device(): pl.pallas_call(pair_kernel, grid=(1,), in_specs=[smem] * 4 + [pl.BlockSpe...  11.8 us
    pallas_call x1, Pallas kernels, on_device(): pl.pallas_call(grid_kernel, grid=(done_steps,), in_specs=[pl.BlockSpec((f...  10.9 us
    ppermute x1, starting transfers between devices, on_device(): lax.ppermute(features[:, :tile], 'blocks', [((i + 1) % owner_total, i) fo...  5.5 us
    unnamed x5, local copies, waits for them, and re-layouts  2.61 us
  transfers between devices with their start and end apart: 2, of which 0 were waited for; matrix products, arithmetic and copies ran while one was open for 0% of the time, Pallas kernels for 13%

profile of v2, /device:TPU:0, one launch (start us, length us, event | category | flops | bytes accessed | tf_op | source)
XLA Modules:
  0.0 84.5 jit_solution(10696844734965209808)
XLA Ops:
  0.6 1.1 %fusion = (bf16[227,512]{1,0:T(8,128)(2,1)S(1)}, bf16[227,512]{1,0:T(8,128)(2,1)S(1)}) fusion(bf16[227,5120]{1,0:T(8,128)(2,1)} %bitcast.9), kind=kLoop, calls=%fused_computation | loop fusion | bytes 929792 | tf_op jit(solution)/shard_map/slice | solution.py:364
  1.7 5.5 %collective-permute-start.1 = (bf16[227,512]{1,0:T(8,128)(2,1)S(1)}, bf16[227,512]{1,0:T(8,128)(2,1)S(1)}, u32[]{:S(2)}, u32[]{:S(2)}) collective-permute-start(bf16[227,512]{1,0:T(8,128)(2,1)S(1)} %get-tuple-element.10), channel_id=1, source_target_pairs={{1,0},{2,1},{3,2},{4,3},{5,4},{6,5},{7,6},{8,7},{9,8},{10,9},{11,1... | collective-permute-start | bytes 697352 | tf_op jit(solution)/shard_map/ppermute | solution.py:363
  7.2 0.0 collective-permute-start
  7.2 10.9 %grid_rows.1 = (bf16[5120,512]{1,0:T(8,128)(2,1)}, bf16[4096,512]{1,0:T(8,128)(2,1)}) custom-call(bf16[227,5120]{1,0:T(8,128)(2,1)} %bitcast.10, bf16[227,512]{1,0:T(8,128)(2,1)} %w_in.3, f32[1,512]{1,0:T(1,128)} %bitcast.12, bf16[512,512]{1,0:T(8,128)(2,1)} %w_out.3, f32[1,512]{1,0:T(1,128)} %bitcast.14, f32[1,512]{1,0:T(1,128)} %bitcast.16, ...), custom_call_target="tpu_custom_call" | custom-call | flops 5247074304 | bytes 10248192 | tf_op jit(solution)/shard_map/grid_rows/pallas_call | solution.py:367
  18.7 0.0 collective-permute-done.1.right
  18.7 0.0 copy-start
  18.8 0.0 collective-permute-done.left
  18.8 0.0 copy-start.1
  18.8 0.7 copy-done
  19.4 0.1 copy-done.1
  19.5 11.8 %pair_sums.1 = (bf16[5120,512]{1,0:T(8,128)(2,1)}, bf16[64,128,512]{2,1,0:T(8,128)(2,1)}) custom-call(s32[1,96]{1,0:T(1,128)} %pair_grid.1, s32[1,96]{1,0:T(1,128)} %pair_slot.1, s32[1,32]{1,0:T(1,128)} %slot_block.1, s32[1]{0:T(128)S(6)} %copy.23.pair_count, bf16[227,5120]{1,0:T(8,128)(2,1)} %bitcast.11, ...), custom_call_target="tpu_custom_call", output_to_operand_aliasing={{0}: (15, {})} | custom-call | tf_op jit(solution)/shard_map/pair_sums/pallas_call | solution.py:388
  31.4 51.2 %ring_sums.1 = bf16[512,512]{1,0:T(8,128)(2,1)} custom-call(bf16[8192,512]{1,0:T(8,128)(2,1)} %bitcast.8, bf16[512,512]{1,0:T(8,128)(2,1)} %mesh_latent.1, bf16[1024,512]{1,0:T(8,128)(2,1)} %w_mesh1.1, f32[1,512]{1,0:T(1,128)} %bitcast.18, bf16[512,512]{1,0:T(8,128)(2,1)} %w_mesh2.1, f32[1,512]{1,0:T(1,128)} %bitcast.19, f32[1,512]{1,0:T(1,128)} %bitcast.20), custom_call_target="tpu_custom_call" | custom-call | tf_op jit(solution)/shard_map/ring_sums/pallas_call | solution.py:430
  82.6 1.9 %copy.24 = bf16[512,512]{1,0:T(8,128)(2,1)} copy(bf16[512,512]{1,0:T(8,128)(2,1)} %ring_sums.1) | data formatting | bytes 1048576
Async XLA Ops:
  1.7 17.0 %collective-permute-start.1 = (bf16[227,512]{1,0:T(8,128)(2,1)S(1)}, bf16[227,512]{1,0:T(8,128)(2,1)S(1)}, u32[]{:S(2)}, u32[]{:S(2)}) collective-permute-start(bf16[227,512]{1,0:T(8,128)(2,1)S(1)} %get-tuple-element.10), channel_id=1, source_target_pairs={{1,0},{2,1},{3,2},{4,3},{5,4},{6,5},{7,6},{8,7},{9,8},{10,9},{11,1... | collective-permute-start | bytes 697352 | tf_op jit(solution)/shard_map/ppermute | solution.py:363
  7.2 11.5 %collective-permute-start = (bf16[227,512]{1,0:T(8,128)(2,1)S(1)}, bf16[227,512]{1,0:T(8,128)(2,1)S(1)}, u32[]{:S(2)}, u32[]{:S(2)}) collective-permute-start(bf16[227,512]{1,0:T(8,128)(2,1)S(1)} %get-tuple-element.11), channel_id=1, source_target_pairs={{0,1},{1,2},{2,3},{3,4},{4,5},{5,6},{6,7},{7,8},{8,9},{9,10},{10,1... | collective-permute-start | bytes 697352 | tf_op jit(solution)/shard_map/ppermute | solution.py:358
  18.7 0.7 copy-start
  18.8 0.7 copy-start.1

commit v3 on v2

--- a/solution.py
+++ b/solution.py
@@ -11,9 +11,11 @@
 cap = 2
 
 norm_eps = 1e-05
-vmem_bytes = 56 * 1024 * 1024
+mib = 1024 * 1024
+grid_mib = 56
+spare_mib = 60
 chain_rows = 128
-unroll = 8
+unroll = 16
 
 
 def silu(values):
@@ -158,17 +160,10 @@
 def ring_kernel(
     device_total,
     sums,
-    mesh_latent,
-    w_mesh1,
-    b_mesh1,
-    w_mesh2,
-    b_mesh2,
-    mesh_gain,
-    mesh_out,
+    aggregate,
     own,
     peer,
     got,
-    hidden,
     own_sem,
     peer_send,
     peer_recv,
@@ -177,7 +172,6 @@
 ):
     chips = device_total // 2
     per_owner = own.shape[1]
-    half = per_owner // 2
     width = own.shape[2]
     chains = per_owner // chain_rows
     me = lax.axis_index("blocks")
@@ -203,27 +197,30 @@
             return chip_at((place + 2 * chips - 1 - step) % chips)
         return chip_at((place + 1 + step) % chips)
 
-    def own_copy(step, way):
-        first = (2 * owner_chip(step, way) + core) * per_owner + way * half
+    def rows_of(chain):
+        return pl.ds(chain * chain_rows, chain_rows)
+
+    def sums_rows(step, chain, which):
+        way = 0 if chain < chains // 2 else 1
+        first = (2 * owner_chip(step, way) + which) * per_owner + chain * chain_rows
+        return sums.at[pl.ds(first, chain_rows)]
+
+    def own_copy(step, chain):
         return pltpu.make_async_copy(
-            sums.at[pl.ds(first, half)],
-            own.at[step, pl.ds(way * half, half)],
-            own_sem.at[step, way],
+            sums_rows(step, chain, core),
+            own.at[step, rows_of(chain)],
+            own_sem.at[step, chain],
         )
 
-    def peer_copy(step, way):
-        first = (2 * owner_chip(step, way) + 1 - core) * per_owner + way * half
+    def peer_copy(step, chain):
         return pltpu.make_async_remote_copy(
-            src_ref=sums.at[pl.ds(first, half)],
-            dst_ref=peer.at[step, pl.ds(way * half, half)],
-            send_sem=peer_send.at[step, way],
-            recv_sem=peer_recv.at[step, way],
+            src_ref=sums_rows(step, chain, 1 - core),
+            dst_ref=peer.at[step, rows_of(chain)],
+            send_sem=peer_send.at[step, chain],
+            recv_sem=peer_recv.at[step, chain],
             device_id={"blocks": other},
             device_id_type=pl.DeviceIdType.MESH,
         )
-
-    def rows_of(chain):
-        return pl.ds(chain * chain_rows, chain_rows)
 
     def ring_copy(step, chain):
         return pltpu.make_async_remote_copy(
@@ -236,76 +233,76 @@
         )
 
     ahead = 3
-
-    @pl.loop(0, chips)
-    def _(step):
-        for way in range(2):
-            own_copy(step, way).start()
-
-    pl.semaphore_wait(barrier, 3)
-    for step in range(ahead):
-        for way in range(2):
-            peer_copy(step, way).start()
-
-    def both(step, chain):
-        rows = rows_of(chain)
-        return own[step, rows].astype(jnp.float32) + peer[step, rows].astype(jnp.float32)
-
-    def arrive(step):
-        for way in range(2):
-            own_copy(step, way).wait()
-            peer_copy(step, way).wait_recv()
-
     order = [
         chain for pair in zip(range(chains // 2), range(chains // 2, chains)) for chain in pair
     ]
-    arrive(0)
+
+    @pl.loop(0, chips)
+    def _(step):
+        for chain in order:
+            own_copy(step, chain).start()
+
+    pl.semaphore_wait(barrier, 3)
+    for step in range(ahead):
+        for chain in order:
+            peer_copy(step, chain).start()
+
+    def both(step, chain):
+        own_copy(step, chain).wait()
+        peer_copy(step, chain).wait_recv()
+        rows = rows_of(chain)
+        return own[step, rows].astype(jnp.float32) + peer[step, rows].astype(jnp.float32)
+
     for chain in order:
         own[0, rows_of(chain)] = both(0, chain).astype(jnp.bfloat16)
         ring_copy(0, chain).start()
-
-    hidden[...] = (
-        jnp.dot(mesh_latent[...], w_mesh1[:width], preferred_element_type=jnp.float32)
-        + b_mesh1[...]
-    )
 
     @pl.loop(1, chips - 1)
     def _(step):
         @pl.when(step + ahead - 1 < chips)
         def _():
-            for way in range(2):
-                peer_copy(step + ahead - 1, way).start()
-
-        arrive(step)
+            for chain in order:
+                peer_copy(step + ahead - 1, chain).start()
+
         for chain in order:
+            held = both(step, chain)
             ring_copy(step - 1, chain).wait_recv()
-            total = both(step, chain) + got[step - 1, rows_of(chain)].astype(jnp.float32)
+            total = held + got[step - 1, rows_of(chain)].astype(jnp.float32)
             own[step, rows_of(chain)] = total.astype(jnp.bfloat16)
             ring_copy(step, chain).start()
 
     last = chips - 1
-    arrive(last)
     for chain in order:
+        held = both(last, chain)
         ring_copy(last - 1, chain).wait_recv()
-        total = both(last, chain) + got[last - 1, rows_of(chain)].astype(jnp.float32)
+        total = held + got[last - 1, rows_of(chain)].astype(jnp.float32)
         rows = rows_of(chain)
-        value = hidden[rows] + jnp.dot(
-            total.astype(jnp.bfloat16), w_mesh1[width:], preferred_element_type=jnp.float32
-        )
-        value = silu(value).astype(jnp.bfloat16)
-        value = jnp.dot(value, w_mesh2[...], preferred_element_type=jnp.float32) + b_mesh2[...]
-        update = layer_norm(value, mesh_gain[...])
-        mesh_out[rows] = (mesh_latent[rows].astype(jnp.float32) + update).astype(jnp.bfloat16)
+        aggregate[rows] = total.astype(jnp.bfloat16)
 
     @pl.loop(0, chips)
     def _(step):
-        for way in range(2):
-            peer_copy(step, way).wait_send()
+        for chain in order:
+            peer_copy(step, chain).wait_send()
 
     @pl.loop(0, chips - 1)
     def _(step):
         for chain in range(chains):
             ring_copy(step, chain).wait_send()
+
+
+def mesh_kernel(
+    aggregate, mesh_latent, w_mesh1, b_mesh1, w_mesh2, b_mesh2, mesh_gain, mesh_out, held, sem
+):
+    width = w_mesh2.shape[0]
+    load = pltpu.make_async_copy(aggregate, held, sem)
+    load.start()
+    value = jnp.dot(mesh_latent[...], w_mesh1[:width], preferred_element_type=jnp.float32)
+    load.wait()
+    value += jnp.dot(held[...], w_mesh1[width:], preferred_element_type=jnp.float32)
+    hidden = silu(value + b_mesh1[...]).astype(jnp.bfloat16)
+    value = jnp.dot(hidden, w_mesh2[...], preferred_element_type=jnp.float32) + b_mesh2[...]
+    update = layer_norm(value, mesh_gain[...])
+    mesh_out[...] = (mesh_latent[...].astype(jnp.float32) + update).astype(jnp.bfloat16)
 
 
 def on_device(
@@ -350,7 +347,7 @@
     wide = 2 * tile
     done_steps = rows // wide - 1
     smem = pl.BlockSpec(memory_space=pltpu.SMEM)
-    anywhere = pl.BlockSpec(memory_space=pl.ANY)
+    anywhere = pl.BlockSpec(memory_space=pltpu.HBM)
     vmem = pl.BlockSpec(memory_space=pltpu.VMEM)
     semaphore = pltpu.SemaphoreType.DMA
     count = done_steps * wide
@@ -381,10 +378,12 @@
             bytes_accessed=count * (feature_width + 2 * width) * 2,
             transcendentals=count * width,
         ),
-        compiler_params=pltpu.CompilerParams(vmem_limit_bytes=vmem_bytes),
+        compiler_params=pltpu.CompilerParams(vmem_limit_bytes=grid_mib * mib),
         name="grid_rows",
     )(features, *params)
 
+    pair_bytes = (rows + 2 * tile + 3 * slot_total * block_size) * width * 2
+    pair_bytes += pair_total * block_size * block_size * 2
     grid_latent, sums = pl.pallas_call(
         pair_kernel,
         grid=(1,),
@@ -409,7 +408,7 @@
             semaphore,
         ],
         input_output_aliases={15: 0},
-        compiler_params=pltpu.CompilerParams(vmem_limit_bytes=vmem_bytes),
+        compiler_params=pltpu.CompilerParams(vmem_limit_bytes=min(56 * mib, pair_bytes + spare_mib * mib)),
         name="pair_sums",
     )(
         pair_grid,
@@ -427,27 +426,35 @@
 
     chips = owner_total // 2
     mesh_rows = own_blocks * block_size
-    mesh_out = pl.pallas_call(
+    aggregate = pl.pallas_call(
         functools.partial(ring_kernel, owner_total),
-        in_specs=[anywhere] + [vmem] * 6,
+        in_specs=[anywhere],
         out_specs=vmem,
         out_shape=jax.ShapeDtypeStruct(mesh_latent.shape, bf16),
         scratch_shapes=[
             pltpu.VMEM((chips, mesh_rows, width), bf16),
             pltpu.VMEM((chips, mesh_rows, width), bf16),
             pltpu.VMEM((chips - 1, mesh_rows, width), bf16),
-            pltpu.VMEM(mesh_latent.shape, f32),
-            pltpu.SemaphoreType.DMA((chips, 2)),
-            pltpu.SemaphoreType.DMA((chips, 2)),
-            pltpu.SemaphoreType.DMA((chips, 2)),
+            pltpu.SemaphoreType.DMA((chips, mesh_rows // chain_rows)),
+            pltpu.SemaphoreType.DMA((chips, mesh_rows // chain_rows)),
+            pltpu.SemaphoreType.DMA((chips, mesh_rows // chain_rows)),
             pltpu.SemaphoreType.DMA((chips - 1, mesh_rows // chain_rows)),
             pltpu.SemaphoreType.DMA((chips - 1, mesh_rows // chain_rows)),
         ],
         compiler_params=pltpu.CompilerParams(
-            collective_id=0, has_side_effects=True, vmem_limit_bytes=vmem_bytes
+            collective_id=0, has_side_effects=True, vmem_limit_bytes=56 * mib
         ),
         name="ring_sums",
-    )(sums.reshape(-1, width), mesh_latent, w_mesh1, flat(b_mesh1), w_mesh2, flat(b_mesh2), flat(mesh_gain))
+    )(sums.reshape(-1, width))
+    mesh_out = pl.pallas_call(
+        mesh_kernel,
+        in_specs=[anywhere] + [vmem] * 6,
+        out_specs=vmem,
+        out_shape=jax.ShapeDtypeStruct(mesh_latent.shape, bf16),
+        scratch_shapes=[pltpu.VMEM(mesh_latent.shape, bf16), semaphore],
+        compiler_params=pltpu.CompilerParams(vmem_limit_bytes=16 * mib),
+        name="mesh_rows",
+    )(aggregate, mesh_latent, w_mesh1, flat(b_mesh1), w_mesh2, flat(b_mesh2), flat(mesh_gain))
     return (grid_latent, mesh_out)
 
 

time: 83.9 us -> 81.8 us (0.975); the launches traced: 84.5 us -> 80.7 us
  Pallas kernels: 73.9 us -> 70.9 us
    pallas_call x1, Pallas kernels: 51.2 us -> 47 us  [on_device(): pl.pallas_call(functools.partial(ring_kernel, owner_total), in_specs=[any...]
    pallas_call x0 -> x1, Pallas kernels: none -> 2.23 us  [on_device(): pl.pallas_call(mesh_kernel, in_specs=[anywhere] + [vmem] * 6, out_specs=v...]
    pallas_call x1, Pallas kernels: 11.8 us -> 10.8 us  [on_device(): pl.pallas_call(pair_kernel, grid=(1,), in_specs=[smem] * 4 + [pl.BlockSpe...]
    unnamed x5 -> x18, local copies, waits for them, and re-layouts: 2.61 us -> 1.81 us
where the time goes in v3:
time: 81.8 us; the launch traced here: 80.7 us
  Pallas kernels  70.9 us (87%)
  starting transfers between devices  5.5 us (7%)
  local copies, waits for them, and re-layouts  2.91 us (4%)
  between operations  1.44 us (2%)
    pallas_call x1, Pallas kernels, on_device(): pl.pallas_call(functools.partial(ring_kernel, owner_total), in_specs=[any...  47 us
    pallas_call x1, Pallas kernels, on_device(): pl.pallas_call(grid_kernel, grid=(done_steps,), in_specs=[pl.BlockSpec((f...  10.9 us
    pallas_call x1, Pallas kernels, on_device(): pl.pallas_call(pair_kernel, grid=(1,), in_specs=[smem] * 4 + [pl.BlockSpe...  10.8 us
    ppermute x1, starting transfers between devices, on_device(): lax.ppermute(features[:, :tile], 'blocks', [((i + 1) % owner_total, i) fo...  5.5 us
    pallas_call x1, Pallas kernels, on_device(): pl.pallas_call(mesh_kernel, in_specs=[anywhere] + [vmem] * 6, out_specs=v...  2.23 us
    unnamed x18, local copies, waits for them, and re-layouts  1.81 us
  transfers between devices with their start and end apart: 2, of which 0 were waited for; matrix products, arithmetic and copies ran while one was open for 0% of the time, Pallas kernels for 13%

profile of v3, /device:TPU:0, one launch (start us, length us, event | category | flops | bytes accessed | tf_op | source)
XLA Modules:
  0.0 80.7 jit_solution(3925575387587365099)
XLA Ops:
  0.6 1.1 %fusion = (bf16[227,512]{1,0:T(8,128)(2,1)S(1)}, bf16[227,512]{1,0:T(8,128)(2,1)S(1)}) fusion(bf16[227,5120]{1,0:T(8,128)(2,1)} %bitcast.12), kind=kLoop, calls=%fused_computation | loop fusion | bytes 929792 | tf_op jit(solution)/shard_map/slice | solution.py:361
  1.7 5.5 %collective-permute-start.1 = (bf16[227,512]{1,0:T(8,128)(2,1)S(1)}, bf16[227,512]{1,0:T(8,128)(2,1)S(1)}, u32[]{:S(2)}, u32[]{:S(2)}) collective-permute-start(bf16[227,512]{1,0:T(8,128)(2,1)S(1)} %get-tuple-element.10), channel_id=1, source_target_pairs={{1,0},{2,1},{3,2},{4,3},{5,4},{6,5},{7,6},{8,7},{9,8},{10,9},{11,1... | collective-permute-start | bytes 697352 | tf_op jit(solution)/shard_map/ppermute | solution.py:360
  7.2 0.0 collective-permute-start
  7.2 10.9 %grid_rows.1 = (bf16[5120,512]{1,0:T(8,128)(2,1)}, bf16[4096,512]{1,0:T(8,128)(2,1)}) custom-call(bf16[227,5120]{1,0:T(8,128)(2,1)} %bitcast.13, bf16[227,512]{1,0:T(8,128)(2,1)} %w_in.3, f32[1,512]{1,0:T(1,128)} %bitcast.15, bf16[512,512]{1,0:T(8,128)(2,1)} %w_out.3, f32[1,512]{1,0:T(1,128)} %bitcast.17, f32[1,512]{1,0:T(1,128)} %bitcast.19, ...), custom_call_target="tpu_custom_call" | custom-call | flops 5247074304 | bytes 10248192 | tf_op jit(solution)/shard_map/grid_rows/pallas_call | solution.py:364
  18.7 0.0 collective-permute-done.1.right
  18.8 0.0 copy-start.7
  18.8 0.0 collective-permute-done.left
  18.8 0.0 copy-start.8
  18.8 0.7 copy-done.7
  19.4 0.1 copy-done.8
  19.5 10.8 %pair_sums.1 = (bf16[5120,512]{1,0:T(8,128)(2,1)}, bf16[64,128,512]{2,1,0:T(8,128)(2,1)}) custom-call(s32[1,96]{1,0:T(1,128)} %pair_grid.1, s32[1,96]{1,0:T(1,128)} %pair_slot.1, s32[1,32]{1,0:T(1,128)} %slot_block.1, s32[1]{0:T(128)S(6)} %copy.22.pair_count, bf16[227,5120]{1,0:T(8,128)(2,1)} %bitcast.14, ...), custom_call_target="tpu_custom_call", output_to_operand_aliasing={{0}: (15, {})} | custom-call | tf_op jit(solution)/shard_map/pair_sums/pallas_call | solution.py:387
  30.3 0.0 copy-start.1
  30.3 0.0 copy-start.2
  30.3 0.0 copy-start.3
  30.3 0.0 copy-start.4
  30.3 0.0 copy-start.5
  30.4 0.0 copy-start.6
  30.4 47.0 %ring_sums.1.aggregate = bf16[512,512]{1,0:T(8,128)(2,1)} custom-call(bf16[8192,512]{1,0:T(8,128)(2,1)} %bitcast.11), custom_call_target="tpu_custom_call" | custom-call | tf_op jit(solution)/shard_map/ring_sums/pallas_call | solution.py:429
  77.4 0.0 copy-done.1
  77.4 0.0 copy-done.2
  77.4 0.0 copy-done.3
  77.4 0.0 copy-done.4
  77.4 0.0 copy-done.5
  77.4 0.0 copy-done.6
  77.4 0.0 copy-start
  77.4 1.0 %copy-done = bf16[512,512]{1,0:T(8,128)(2,1)S(1)} copy-done((bf16[512,512]{1,0:T(8,128)(2,1)S(1)}, bf16[512,512]{1,0:T(8,128)(2,1)}, u32[]{:S(2)}) %copy-start) | copy-done | bytes 524312
  78.5 2.2 %mesh_rows.1 = bf16[512,512]{1,0:T(8,128)(2,1)} custom-call(bf16[512,512]{1,0:T(8,128)(2,1)S(1)} %copy-done, bf16[512,512]{1,0:T(8,128)(2,1)S(1)} %copy-done.2, bf16[1024,512]{1,0:T(8,128)(2,1)S(1)} %copy-done.1, f32[1,512]{1,0:T(1,128)S(1)} %bitcast.8, bf16[512,512]{1,0:T(8,128)(2,1)S(1)} %copy-done.3, f32[1,512]{1,0:T(1,128)S(1)} %bitcast.9, ...), custom_call_target="tpu_custom_call" | custom-call | tf_op jit(solution)/shard_map/mesh_rows/pallas_call | solution.py:449
Async XLA Ops:
  1.7 17.0 %collective-permute-start.1 = (bf16[227,512]{1,0:T(8,128)(2,1)S(1)}, bf16[227,512]{1,0:T(8,128)(2,1)S(1)}, u32[]{:S(2)}, u32[]{:S(2)}) collective-permute-start(bf16[227,512]{1,0:T(8,128)(2,1)S(1)} %get-tuple-element.10), channel_id=1, source_target_pairs={{1,0},{2,1},{3,2},{4,3},{5,4},{6,5},{7,6},{8,7},{9,8},{10,9},{11,1... | collective-permute-start | bytes 697352 | tf_op jit(solution)/shard_map/ppermute | solution.py:360
  7.2 11.5 %collective-permute-start = (bf16[227,512]{1,0:T(8,128)(2,1)S(1)}, bf16[227,512]{1,0:T(8,128)(2,1)S(1)}, u32[]{:S(2)}, u32[]{:S(2)}) collective-permute-start(bf16[227,512]{1,0:T(8,128)(2,1)S(1)} %get-tuple-element.11), channel_id=1, source_target_pairs={{0,1},{1,2},{2,3},{3,4},{4,5},{5,6},{6,7},{7,8},{8,9},{9,10},{10,1... | collective-permute-start | bytes 697352 | tf_op jit(solution)/shard_map/ppermute | solution.py:355
  18.8 0.7 copy-start.7
  18.8 0.7 copy-start.8
  30.3 47.1 %copy-start.1 = (bf16[1024,512]{1,0:T(8,128)(2,1)S(1)}, bf16[1024,512]{1,0:T(8,128)(2,1)}, u32[]{:S(2)}) copy-start(bf16[1024,512]{1,0:T(8,128)(2,1)} %w_mesh1.1) | copy-start | bytes 3145732
  30.3 47.1 %copy-start.2 = (bf16[512,512]{1,0:T(8,128)(2,1)S(1)}, bf16[512,512]{1,0:T(8,128)(2,1)}, u32[]{:S(2)}) copy-start(bf16[512,512]{1,0:T(8,128)(2,1)} %mesh_latent.1) | copy-start | bytes 1572868
  30.3 47.1 %copy-start.3 = (bf16[512,512]{1,0:T(8,128)(2,1)S(1)}, bf16[512,512]{1,0:T(8,128)(2,1)}, u32[]{:S(2)}) copy-start(bf16[512,512]{1,0:T(8,128)(2,1)} %w_mesh2.1) | copy-start | bytes 1572868
  30.3 47.1 %copy-start.4 = (f32[512]{0:T(512)S(1)}, f32[512]{0:T(512)}, u32[]{:S(2)}) copy-start(f32[512]{0:T(512)} %param.32) | copy-start | bytes 6148
  30.3 47.1 %copy-start.5 = (f32[512]{0:T(512)S(1)}, f32[512]{0:T(512)}, u32[]{:S(2)}) copy-start(f32[512]{0:T(512)} %param.34) | copy-start | bytes 6148
  30.4 47.1 %copy-start.6 = (f32[512]{0:T(512)S(1)}, f32[512]{0:T(512)}, u32[]{:S(2)}) copy-start(f32[512]{0:T(512)} %param.35) | copy-start | bytes 6148
  77.4 1.0 %copy-start = (bf16[512,512]{1,0:T(8,128)(2,1)S(1)}, bf16[512,512]{1,0:T(8,128)(2,1)}, u32[]{:S(2)}) copy-start(bf16[512,512]{1,0:T(8,128)(2,1)} %ring_sums.1.aggregate) | copy-start | bytes 1572868
